TPU v7x, 32 devices: a whole 2x2x4 slice. The times are simulated.
32 devices in a mesh: groups: 2 (over y), row: 4 (over z), col: 4 (over x, core).
Axes of the slice: x: 2, y: 2, z: 4, core: 2. Of those that a mesh axis runs over, the one named last changes fastest.
Arguments:
- grad_out: bfloat16 [2048, 12288], P(('groups', 'row'), 'col'), parts along dimension 0, may hold values from -6 to 6
- preact: bfloat16 [2048, 24576], P(('groups', 'col'), 'row'), parts along dimension 0, may hold values from -6 to 6
- down_weight: bfloat16 [24576, 12288], P('row', 'col'), may hold values from -0.0546875 to 0.0546875
- sketch_matrix: bfloat16 [24576, 512], P('row'), may hold values from -0.0017089844 to 0.0017089844
Outputs:
- grad_pre: bfloat16 [2048, 24576], P(('groups', 'col'), 'row'), parts along dimension 0
- sketch: float32 [1024, 12288], P(('groups', 'row'), 'col'), parts along dimension 0
There are 2 independent parts, one for each index of `groups`. A program takes and returns all parts, laid end to end along the dimension named above; an argument that names none is the same for every part. Nothing has to cross between parts.
All inputs are finite; a program needn't handle non-finite values.
Results may differ from a plain program's by a relative error of at most 0.011.
Values may be sent and summed in bfloat16 or wider, within the bound.
A program may use at most 192 MiB of HBM per device.

v0:
```python
import jax
import jax.numpy as jnp
from jax import lax
from jax.sharding import PartitionSpec as P

gelu_scale = 0.7978845608028654
cubic_term = 0.044715


def gelu_parts(preact):
    pre_f32 = preact.astype(jnp.float32)
    inner_arg = gelu_scale * (pre_f32 + cubic_term * pre_f32 * pre_f32 * pre_f32)
    tangent = jnp.tanh(inner_arg)
    value = 0.5 * pre_f32 * (1.0 + tangent)
    slope = 0.5 * (1.0 + tangent) + 0.5 * pre_f32 * (1.0 - tangent * tangent) * gelu_scale * (
        1.0 + 3.0 * cubic_term * pre_f32 * pre_f32
    )
    return (value, slope)


def per_device(grad_out, preact, down_weight, sketch_matrix):
    grad_rows = lax.all_gather(grad_out, "row", axis=0, tiled=True)
    hidden_grad = lax.psum_scatter(
        lax.dot_general(
            grad_rows, down_weight, (((1,), (1,)), ((), ())), preferred_element_type=jnp.float32
        ).astype(jnp.bfloat16),
        "col",
        scatter_dimension=0,
        tiled=True,
    ).astype(jnp.float32)
    value, slope = gelu_parts(preact)
    grad_pre = (hidden_grad * slope).astype(jnp.bfloat16)
    act_local = value.astype(jnp.bfloat16)
    act_every = lax.all_gather(act_local, "col", axis=0, tiled=True)
    reduced = lax.psum_scatter(
        lax.dot_general(
            sketch_matrix, act_every, (((0,), (1,)), ((), ())), preferred_element_type=jnp.float32
        ).astype(jnp.bfloat16),
        "row",
        scatter_dimension=0,
        tiled=True,
    ).astype(jnp.float32)
    sketch = jnp.dot(
        reduced,
        grad_rows.astype(jnp.float32),
        precision=lax.Precision.HIGHEST,
        preferred_element_type=jnp.float32,
    )
    return (grad_pre, sketch)


def solution(mesh):
    in_specs = (
        P(("groups", "row"), "col"),
        P(("groups", "col"), "row"),
        P("row", "col"),
        P("row", None),
    )
    out_specs = (P(("groups", "col"), "row"), P(("groups", "row"), "col"))
    return jax.shard_map(
        per_device, mesh=mesh, in_specs=in_specs, out_specs=out_specs, check_vma=False
    )
```

profile of v0, /device:TPU:0, one launch (start us, length us, event | category | flops | bytes accessed | tf_op | source)
XLA Modules:
  0.0 413.0 jit_solution(18400250298376004255)
XLA Ops:
  7.2 0.0 all-gather.3.cloned.1.call-start
  7.2 0.7 all-gather.3.cloned.1.call-update
  7.9 0.0 reduce-scatter.5.cloned.1.call-start
  7.9 119.7 %all-gather.3.cloned.1.call-done = bf16[1024,3072]{1,0:T(8,128)(2,1)} async-done(((bf16[256,3072]{1,0:T(8,128)(2,1)}), bf16[1024,3072]{1,0:T(8,128)(2,1)}) %all-gather.3.cloned.1.call-update) | async-done | bytes 6291472 | tf_op jit(solution)/shard_map/all_gather | solution.py:22
  127.7 46.2 %convolution_convert_fusion = bf16[1024,6144]{1,0:T(8,128)(2,1)} fusion(bf16[1024,3072]{1,0:T(8,128)(2,1)} %all-gather.3.cloned.1.call-done, bf16[6144,3072]{1,0:T(8,128)(2,1)} %param.6), kind=kOutput, calls=%fused_computation.7 | convolution fusion | flops 38660997120 | bytes 56623104 | tf_op jit(solution)/shard_map/dot_general | solution.py:24
  173.8 0.0 copy-start
  173.8 0.0 reduce-scatter.5.cloned.1.call-update
  173.8 0.0 all-gather.5.cloned.1.call-start
  173.9 97.4 %reduce-scatter.5.cloned.1.call-done = bf16[256,6144]{1,0:T(8,128)(2,1)} async-done(((bf16[1024,6144]{1,0:T(8,128)(2,1)}), bf16[256,6144]{1,0:T(8,128)(2,1)}) %reduce-scatter.5.cloned.1.call-update) | async-done | bytes 3145744 | tf_op jit(solution)/shard_map/reduce_scatter | solution.py:23
  271.3 0.0 copy-done
  271.3 7.8 %fusion.7 = (bf16[256,6144]{1,0:T(8,128)(2,1)}, bf16[256,6144]{1,0:T(8,128)(2,1)}) fusion(bf16[256,6144]{1,0:T(8,128)(2,1)S(1)} %copy-done, bf16[256,6144]{1,0:T(8,128)(2,1)} %reduce-scatter.5.cloned.1.call-done), kind=kLoop, calls=%fused_computation.15 | loop fusion | flops 36175872 | bytes 12582912 | tf_op jit(solution)/shard_map/convert_element_type | solution.py:33
  279.1 0.0 all-gather.5.cloned.1.call-update
  279.1 0.0 reduce-scatter.7.cloned.1.call-start
  279.1 82.2 %all-gather.5.cloned.1.call-done = bf16[1024,6144]{1,0:T(8,128)(2,1)} async-done(((bf16[256,6144]{1,0:T(8,128)(2,1)}), bf16[1024,6144]{1,0:T(8,128)(2,1)}) %all-gather.5.cloned.1.call-update) | async-done | bytes 12582928 | tf_op jit(solution)/shard_map/all_gather | solution.py:34
  361.3 11.4 %fusion.11 = bf16[512,1024]{0,1:T(8,128)(2,1)S(1)} fusion(bf16[1024,6144]{1,0:T(8,128)(2,1)} %all-gather.5.cloned.1.call-done, bf16[6144,512]{1,0:T(8,128)(2,1)} %param.7), kind=kOutput, calls=%fused_computation.20 | convolution fusion | flops 6442975232 | bytes 19922944 | tf_op jit(solution)/shard_map/dot_general | solution.py:36
  372.8 1.3 copy.6
  374.1 0.0 reduce-scatter.7.cloned.1.call-update
  374.1 27.3 %reduce-scatter.7.cloned.1.call-done = bf16[128,1024]{1,0:T(8,128)(2,1)} async-done(((bf16[512,1024]{1,0:T(8,128)(2,1)}), bf16[128,1024]{1,0:T(8,128)(2,1)}) %reduce-scatter.7.cloned.1.call-update) | async-done | bytes 262160
  401.4 5.0 %fusion.12 = f32[128,3072]{1,0:T(8,128)} fusion(bf16[128,1024]{1,0:T(8,128)(2,1)} %reduce-scatter.7.cloned.1.call-done, bf16[1024,3072]{1,0:T(8,128)(2,1)} %all-gather.3.cloned.1.call-done), kind=kOutput, calls=%fused_computation.21 | convolution fusion | flops 805306368 | bytes 8126464 | tf_op jit(solution)/shard_map/dot_general | solution.py:43
Async XLA Ops:
  7.2 120.5 %all-gather.3.cloned.1.call-start = ((), (), s32[]{:S(2)}) async-start(), calls=%async_computation.2 | async-start | bytes 7864320 | tf_op jit(solution)/shard_map/all_gather | solution.py:22
  7.9 263.4 %reduce-scatter.5.cloned.1.call-start = ((), (), s32[]{:S(2)}) async-start(), calls=%async_computation.3 | async-start | bytes 15728640 | tf_op jit(solution)/shard_map/reduce_scatter | solution.py:23
  173.8 97.5 %copy-start = (bf16[256,6144]{1,0:T(8,128)(2,1)S(1)}, bf16[256,6144]{1,0:T(8,128)(2,1)}, u32[]{:S(2)}) copy-start(bf16[256,6144]{1,0:T(8,128)(2,1)} %param.5) | copy-start | bytes 9437188
  173.8 187.5 %all-gather.5.cloned.1.call-start = ((), (), s32[]{:S(2)}) async-start(), calls=%async_computation.4 | async-start | bytes 15728640 | tf_op jit(solution)/shard_map/all_gather | solution.py:34
  279.1 122.4 %reduce-scatter.7.cloned.1.call-start = ((), (), s32[]{:S(2)}) async-start(), calls=%async_computation.5 | async-start | bytes 1310720
Sparse Core Ops, SparseCore 0:
  9.6 118.0 all-gather.2
  174.0 97.2 reduce-scatter.4
  279.2 82.1 all-gather.4
  374.3 27.1 reduce-scatter.6
where the time goes:
time: 413 us
  waiting for transfers between devices  327 us (79%)
  matrix products  62.6 us (15%)
  between operations  13.8 us (3%)
  other arithmetic  7.78 us (2%)
    all_gather x1, waiting for transfers between devices, per_device(): grad_rows = lax.all_gather(grad_out, 'row', axis=0, tiled=True)  120 us
    reduce_scatter x1, waiting for transfers between devices, per_device(): lax.psum_scatter(lax.dot_general(grad_rows, down_weight, (((1,), (1,)), (...  97.4 us
    all_gather x1, waiting for transfers between devices, per_device(): act_every = lax.all_gather(act_local, 'col', axis=0, tiled=True)  82.2 us
    dot_general x1, matrix products, per_device(): lax.dot_general(grad_rows, down_weight, (((1,), (1,)), ((), ())), preferr...  46.2 us
    unnamed x5, waiting for transfers between devices  28 us
    dot_general x1, matrix products, per_device(): lax.dot_general(sketch_matrix, act_every, (((0,), (1,)), ((), ())), prefe...  11.4 us
  transfers between devices with their start and end apart: 4, of which 4 were waited for; matrix products, arithmetic and copies ran while one was open for 0% of the time, Pallas kernels for 0%

commit v1 on v0

--- a/solution.py
+++ b/solution.py
@@ -19,7 +19,12 @@
 
 
 def per_device(grad_out, preact, down_weight, sketch_matrix):
-    grad_rows = lax.all_gather(grad_out, "row", axis=0, tiled=True)
+    ring = [grad_out]
+    for hop in range(3):
+        ring.append(lax.ppermute(ring[-1], "row", [(dev, (dev + 1) % 4) for dev in range(4)]))
+    grad_rows = jnp.roll(
+        jnp.concatenate(ring[::-1], axis=0), (lax.axis_index("row") + 1) * ring[0].shape[0], axis=0
+    )
     hidden_grad = lax.psum_scatter(
         lax.dot_general(
             grad_rows, down_weight, (((1,), (1,)), ((), ())), preferred_element_type=jnp.float32

time: 413 us -> 422 us (1.022)
  local copies, waits for them, and re-layouts: 1.32 us -> 17.1 us
  waiting for transfers between devices: 327 us -> 317 us
    all_gather x1 -> x0, waiting for transfers between devices: 120 us -> none  [per_device(): grad_rows = lax.all_gather(grad_out, 'row', axis=0, tiled=True)]
    ppermute x0 -> x3, waiting for transfers between devices: none -> 111 us  [per_device(): lax.ppermute(ring[-1], 'row', [(dev, (dev + 1) % 4) for dev in range(4)])]
    unnamed x3 -> x12, local copies, waits for them, and re-layouts: 1.32 us -> 15.8 us
    unnamed x5 -> x4, waiting for transfers between devices: 28 us -> 27.3 us
  transfers between devices with their start and end apart: 4 -> 6, of which waited for: 4 -> 6; matrix products, arithmetic and copies ran while one was open for 0% -> 0% of each run, Pallas kernels for 0% -> 0%
where the time goes in v1:
time: 422 us
  waiting for transfers between devices  317 us (75%)
  matrix products  62.6 us (15%)
  local copies, waits for them, and re-layouts  17.1 us (4%)
  between operations  13.8 us (3%)
  other arithmetic  7.78 us (2%)
    ppermute x3, waiting for transfers between devices, per_device(): lax.ppermute(ring[-1], 'row', [(dev, (dev + 1) % 4) for dev in range(4)])  111 us
    reduce_scatter x1, waiting for transfers between devices, per_device(): lax.psum_scatter(lax.dot_general(grad_rows, down_weight, (((1,), (1,)), (...  96.9 us
    all_gather x1, waiting for transfers between devices, per_device(): act_every = lax.all_gather(act_local, 'col', axis=0, tiled=True)  82 us
    dot_general x1, matrix products, per_device(): lax.dot_general(grad_rows, down_weight, (((1,), (1,)), ((), ())), preferr...  46.2 us
    unnamed x4, waiting for transfers between devices  27.3 us
    unnamed x12, local copies, waits for them, and re-layouts  15.8 us
    dot_general x1, matrix products, per_device(): lax.dot_general(sketch_matrix, act_every, (((0,), (1,)), ((), ())), prefe...  11.4 us
  transfers between devices with their start and end apart: 6, of which 6 were waited for; matrix products, arithmetic and copies ran while one was open for 0% of the time, Pallas kernels for 0%

profile of v1, /device:TPU:0, one launch (start us, length us, event | category | flops | bytes accessed | tf_op | source)
XLA Modules:
  0.0 421.8 jit_solution(2622507871512398455)
XLA Ops:
  7.2 0.0 reduce-scatter.5.cloned.1.call-start
  7.2 3.1 collective-permute-start
  10.3 36.6 %collective-permute-done = bf16[256,3072]{1,0:T(8,128)(2,1)S(1)} collective-permute-done((bf16[256,3072]{1,0:T(8,128)(2,1)}, bf16[256,3072]{1,0:T(8,128)(2,1)S(1)}, u32[]{:S(2)}, u32[]{:S(2)}) %collective-permute-start) | collective-permute-done | bytes 1572896 | tf_op jit(solution)/shard_map/ppermute | solution.py:24
  46.9 37.5 %collective-permute-done.1 = bf16[256,3072]{1,0:T(8,128)(2,1)} collective-permute-done((bf16[256,3072]{1,0:T(8,128)(2,1)S(1)}, bf16[256,3072]{1,0:T(8,128)(2,1)}, u32[]{:S(2)}, u32[]{:S(2)}) %collective-permute-start.1) | collective-permute-done | bytes 1572896 | tf_op jit(solution)/shard_map/ppermute | solution.py:24
  84.4 36.8 %collective-permute-done.2 = bf16[256,3072]{1,0:T(8,128)(2,1)} collective-permute-done((bf16[256,3072]{1,0:T(8,128)(2,1)}, bf16[256,3072]{1,0:T(8,128)(2,1)}, u32[]{:S(2)}, u32[]{:S(2)}) %collective-permute-start.2) | collective-permute-done | bytes 1572896 | tf_op jit(solution)/shard_map/ppermute | solution.py:24
  121.2 2.7 constant_dynamic-update-slice_fusion.7
  123.9 2.6 constant_dynamic-update-slice_fusion.6
  126.5 1.2 constant_dynamic-update-slice_fusion.5
  127.8 1.3 constant_dynamic-update-slice_fusion.4
  129.0 2.7 constant_dynamic-update-slice_fusion.3
  131.7 2.6 constant_dynamic-update-slice_fusion.2
  134.4 1.3 constant_dynamic-update-slice_fusion.1
  135.7 1.3 constant_dynamic-update-slice_fusion
  136.9 46.2 %convolution_convert_fusion = bf16[1024,6144]{1,0:T(8,128)(2,1)} fusion(bf16[6144,3072]{1,0:T(8,128)(2,1)} %param.6, bf16[2048,3072]{1,0:T(8,128)(2,1)} %constant_dynamic-update-slice_fusion, s32[]{:T(128)S(6)} %select_n.14), kind=kOutput, calls=%fused_computation.7 | convolution fusion | flops 38660997120 | bytes 56623108 | tf_op jit(solution)/shard_map/dot_general | solution.py:29
  183.1 0.0 reduce-scatter.5.cloned.1.call-update
  183.1 0.0 all-gather.2.cloned.1.call-start
  183.2 96.9 %reduce-scatter.5.cloned.1.call-done = bf16[256,6144]{1,0:T(8,128)(2,1)} async-done(((bf16[1024,6144]{1,0:T(8,128)(2,1)}), bf16[256,6144]{1,0:T(8,128)(2,1)}) %reduce-scatter.5.cloned.1.call-update) | async-done | bytes 3145744 | tf_op jit(solution)/shard_map/reduce_scatter | solution.py:28
  280.1 7.8 %fusion.7 = (bf16[256,6144]{1,0:T(8,128)(2,1)}, bf16[256,6144]{1,0:T(8,128)(2,1)}) fusion(bf16[256,6144]{1,0:T(8,128)(2,1)S(1)} %copy-done.1, bf16[256,6144]{1,0:T(8,128)(2,1)} %reduce-scatter.5.cloned.1.call-done), kind=kLoop, calls=%fused_computation.15 | loop fusion | flops 36175872 | bytes 12582912 | tf_op jit(solution)/shard_map/convert_element_type | solution.py:38
  287.9 0.2 reduce-scatter.7.cloned.1.call-start
  288.1 82.0 %all-gather.2.cloned.1.call-done = bf16[1024,6144]{1,0:T(8,128)(2,1)} async-done(((bf16[256,6144]{1,0:T(8,128)(2,1)}), bf16[1024,6144]{1,0:T(8,128)(2,1)}) %all-gather.2.cloned.1.call-update) | async-done | bytes 12582928 | tf_op jit(solution)/shard_map/all_gather | solution.py:39
  370.2 11.4 %fusion.14 = bf16[512,1024]{0,1:T(8,128)(2,1)S(1)} fusion(bf16[1024,6144]{1,0:T(8,128)(2,1)} %all-gather.2.cloned.1.call-done, bf16[6144,512]{1,0:T(8,128)(2,1)} %param.7), kind=kOutput, calls=%fused_computation.23 | convolution fusion | flops 6442975232 | bytes 19922944 | tf_op jit(solution)/shard_map/dot_general | solution.py:41
  381.6 1.3 copy.6
  382.9 27.3 %reduce-scatter.7.cloned.1.call-done = bf16[128,1024]{1,0:T(8,128)(2,1)} async-done(((bf16[512,1024]{1,0:T(8,128)(2,1)}), bf16[128,1024]{1,0:T(8,128)(2,1)}) %reduce-scatter.7.cloned.1.call-update) | async-done | bytes 262160
  410.2 5.0 %fusion.11 = f32[128,3072]{1,0:T(8,128)} fusion(bf16[128,1024]{1,0:T(8,128)(2,1)} %reduce-scatter.7.cloned.1.call-done, bf16[2048,3072]{1,0:T(8,128)(2,1)} %constant_dynamic-update-slice_fusion, s32[]{:T(128)S(6)} %select_n.14), kind=kOutput, calls=%fused_computation.19 | convolution fusion | flops 805306368 | bytes 8126468 | tf_op jit(solution)/shard_map/dot_general | solution.py:48
  (8 shorter events, 0.0 us)
Async XLA Ops:
  7.2 120.6 %copy-start = (bf16[256,3072]{1,0:T(8,128)(2,1)S(1)}, bf16[256,3072]{1,0:T(8,128)(2,1)}, u32[]{:S(2)}) copy-start(bf16[256,3072]{1,0:T(8,128)(2,1)} %param.4) | copy-start | bytes 4718596
  7.2 272.9 %reduce-scatter.5.cloned.1.call-start = ((), (), s32[]{:S(2)}) async-start(), calls=%async_computation.2 | async-start | bytes 15728640 | tf_op jit(solution)/shard_map/reduce_scatter | solution.py:28
  7.2 39.7 %collective-permute-start = (bf16[256,3072]{1,0:T(8,128)(2,1)}, bf16[256,3072]{1,0:T(8,128)(2,1)S(1)}, u32[]{:S(2)}, u32[]{:S(2)}) collective-permute-start(bf16[256,3072]{1,0:T(8,128)(2,1)} %param.4), channel_id=1, source_target_pairs={{0,4},{4,8},{8,12},{12,0},{1,5},{5,9},{9,13},{13,1},{2,6},{6,10},{... | collective-permute-start | bytes 4718600 | tf_op jit(solution)/shard_map/ppermute | solution.py:24
  46.9 37.5 %collective-permute-start.1 = (bf16[256,3072]{1,0:T(8,128)(2,1)S(1)}, bf16[256,3072]{1,0:T(8,128)(2,1)}, u32[]{:S(2)}, u32[]{:S(2)}) collective-permute-start(bf16[256,3072]{1,0:T(8,128)(2,1)S(1)} %collective-permute-done), channel_id=1, source_target_pairs={{0,4},{4,8},{8,12},{12,0},{1,5},{5,9},{9,13},{13,1},{2,6},{6,10},{... | collective-permute-start | bytes 4718600 | tf_op jit(solution)/shard_map/ppermute | solution.py:24
  84.4 36.8 %collective-permute-start.2 = (bf16[256,3072]{1,0:T(8,128)(2,1)}, bf16[256,3072]{1,0:T(8,128)(2,1)}, u32[]{:S(2)}, u32[]{:S(2)}) collective-permute-start(bf16[256,3072]{1,0:T(8,128)(2,1)} %collective-permute-done.1), channel_id=1, source_target_pairs={{0,4},{4,8},{8,12},{12,0},{1,5},{5,9},{9,13},{13,1},{2,6},{6,10},{... | collective-permute-start | bytes 4718600 | tf_op jit(solution)/shard_map/ppermute | solution.py:24
  183.1 97.0 %copy-start.1 = (bf16[256,6144]{1,0:T(8,128)(2,1)S(1)}, bf16[256,6144]{1,0:T(8,128)(2,1)}, u32[]{:S(2)}) copy-start(bf16[256,6144]{1,0:T(8,128)(2,1)} %param.5) | copy-start | bytes 9437188
  183.1 187.0 %all-gather.2.cloned.1.call-start = ((), (), s32[]{:S(2)}) async-start(), calls=%async_computation.3 | async-start | bytes 15728640 | tf_op jit(solution)/shard_map/all_gather | solution.py:39
  287.9 122.4 %reduce-scatter.7.cloned.1.call-start = ((), (), s32[]{:S(2)}) async-start(), calls=%async_computation.4 | async-start | bytes 1310720
Sparse Core Ops, SparseCore 0:
  183.2 96.7 reduce-scatter.4
  288.0 82.0 all-gather.1
  383.1 27.1 reduce-scatter.6
